TPU v7x, 512 devices: a whole 4x8x8 slice. The times are simulated.
512 devices in a mesh: tm: 64 (over z, y), panel: 8 (over x, core).
Axes of the slice: x: 4, y: 8, z: 8, core: 2. Of those that a mesh axis runs over, the one named last changes fastest.
Arguments:
- factor_inverse: float32 [64, 768, 768], P('tm', None, 'panel'), may hold values from -1 to 1, as said below
- coupling: float32 [64, 768, 768], P('tm', None, 'panel'), may hold values from -1 to 1
- sigma_after: float32 [768, 768], replicated, may hold values from -1 to 3, as said below
Outputs:
- marginal_cov: float32 [64, 768, 768], P('tm', None, 'panel')
- propagator: bfloat16 [64, 768, 768], P('tm', None, 'panel')
Inputs may be any that keep to these rules, and one draw needn't show every extreme that they name: `factor_inverse`: factor_inverse_t is lower triangular with a positive diagonal. sigma_after is symmetric.
All inputs are finite; a program needn't handle non-finite values.
Results may differ from a plain program's by a relative error of at most 0.007.
The roundings to bfloat16 on the way count: a program that leaves them out, or rounds other values in their place, can miss the bound.
Values may be sent and summed in bfloat16 or wider, within the bound.
A program may use at most 64 MiB of HBM per device.

v0:
```python
import jax
import jax.numpy as jnp
from jax import lax
from jax.sharding import PartitionSpec as P


def passed_along(block, axis, distance):
    devices = range(lax.axis_size(axis))
    route = [(i - distance, i) for i in devices if i - distance in devices]
    return lax.ppermute(block, axis, route)


def shards(factor_inverse, coupling, sigma_after):
    highest = lax.Precision.HIGHEST
    steps_tm = lax.axis_size("tm")
    where_tm = lax.axis_index("tm")
    panel_width = factor_inverse.shape[2]
    panel_start = lax.axis_index("panel") * panel_width
    factor_cols = factor_inverse[0]
    base_cols = lax.dot_general(
        lax.all_gather(factor_cols.astype(jnp.bfloat16), "panel", axis=1, tiled=True).astype(
            jnp.float32
        ),
        factor_cols,
        (((0,), (0,)), ((), ())),
        precision=highest,
        preferred_element_type=jnp.float32,
    )
    own_part = coupling[0].astype(jnp.bfloat16)
    full_coupling = lax.all_gather(own_part, "panel", axis=1, tiled=True)
    is_last = where_tm == steps_tm - 1
    exact_coupling = full_coupling.astype(jnp.float32)
    weighted = jnp.dot(sigma_after, own_part.astype(jnp.float32), precision=highest)
    folded = lax.dot_general(exact_coupling, weighted, (((0,), (0,)), ((), ())), precision=highest)
    covariance = base_cols + jnp.where(is_last, folded, jnp.zeros_like(folded))
    composite = full_coupling
    final_cols = own_part
    rounds = (steps_tm - 1).bit_length()
    for round_bit in range(rounds):
        distance = 1 << round_bit
        keep_going = round_bit + 1 < rounds
        share_bf = covariance.astype(jnp.bfloat16)
        own_cols = lax.dynamic_slice_in_dim(composite, panel_start, panel_width, 1)
        incoming = passed_along(share_bf, "tm", -distance)
        partner_comp = passed_along(composite, "tm", -distance)
        partner_cov = lax.all_gather(incoming, "panel", axis=1, tiled=True)
        middle = jnp.dot(partner_cov, own_cols, preferred_element_type=jnp.float32).astype(
            jnp.bfloat16
        )
        update = lax.dot_general(
            composite, middle, (((0,), (0,)), ((), ())), preferred_element_type=jnp.float32
        )
        active = where_tm + distance < steps_tm
        covariance = jnp.where(active, covariance + update, covariance)
        if keep_going:
            extended_complement = jnp.dot(
                partner_comp, composite, preferred_element_type=jnp.float32
            ).astype(jnp.bfloat16)
            composite = jnp.where(active, extended_complement, composite)
        else:
            extended_cols = jnp.dot(
                partner_comp, own_cols, preferred_element_type=jnp.float32
            ).astype(jnp.bfloat16)
            final_cols = jnp.where(active, extended_cols, own_cols)
    return (covariance[None], final_cols[None])


def solution(mesh):
    placed = (P("tm", None, "panel"), P("tm", None, "panel"), P())
    return jax.shard_map(
        shards,
        mesh=mesh,
        in_specs=placed,
        out_specs=(P("tm", None, "panel"), P("tm", None, "panel")),
        check_vma=False,
    )
```

profile of v0, /device:TPU:151, one launch (start us, length us, event | category | flops | bytes accessed | tf_op | source)
XLA Modules:
  0.0 518.8 jit_solution(9636990020363920412)
XLA Ops:
  12.9 28.5 %all-gather.24.cloned.1.call-done = bf16[1,768,768]{1,2,0:T(8,128)(2,1)} async-done(((bf16[1,768,96]{1,2,0:T(8,128)(2,1)}), bf16[1,768,768]{1,2,0:T(8,128)(2,1)}) %all-gather.24.cloned.1.call-update) | async-done | bytes 1179664 | tf_op jit(solution)/shard_map/all_gather | solution.py:30
  41.4 3.2 fusion.10
  44.6 28.0 %all-gather.10.cloned.1.call-done = bf16[768,768]{0,1:T(8,128)(2,1)} async-done(((bf16[768,96]{0,1:T(8,128)(2,1)}), bf16[768,768]{0,1:T(8,128)(2,1)}) %all-gather.10.cloned.1.call-update) | async-done | bytes 1179664 | tf_op jit(solution)/shard_map/all_gather | solution.py:21
  72.6 3.3 fusion.50
  78.1 5.0 collective-permute-done
  83.2 30.0 %all-gather.12.cloned.1.call-done = bf16[768,768]{0,1:T(8,128)(2,1)} async-done(((bf16[768,96]{0,1:T(8,128)(2,1)}), bf16[768,768]{0,1:T(8,128)(2,1)}) %all-gather.12.cloned.1.call-update) | async-done | bytes 1179664 | tf_op jit(solution)/shard_map/all_gather | solution.py:46
  113.2 3.5 fusion.51
  118.8 10.5 %collective-permute-done.2 = bf16[768,96]{0,1:T(8,128)(2,1)} collective-permute-done((bf16[768,96]{0,1:T(8,128)(2,1)}, bf16[768,96]{0,1:T(8,128)(2,1)}, u32[]{:S(2)}, u32[]{:S(2)}) %collective-permute-start.2) | collective-permute-done | bytes 147488 | tf_op jit(solution)/shard_map/ppermute | solution.py:10
  131.3 26.4 %collective-permute-done.1 = bf16[768,768]{0,1:T(8,128)(2,1)} collective-permute-done((bf16[768,768]{0,1:T(8,128)(2,1)S(1)}, bf16[768,768]{0,1:T(8,128)(2,1)}, u32[]{:S(2)}, u32[]{:S(2)}) %collective-permute-start.1) | collective-permute-done | bytes 1179680 | tf_op jit(solution)/shard_map/ppermute | solution.py:10
  157.7 3.4 fusion
  161.1 4.0 fusion.54
  165.1 7.2 %collective-permute-start.4 = (bf16[768,96]{0,1:T(8,128)(2,1)}, bf16[768,96]{0,1:T(8,128)(2,1)}, u32[]{:S(2)}, u32[]{:S(2)}) collective-permute-start(bf16[768,96]{0,1:T(8,128)(2,1)} %get-tuple-element.6), channel_id=1, source_target_pairs={{32,0},{40,8},{48,16},{56,24},{64,32},{72,40},{80,48},{88,56},{96,... | collective-permute-start | bytes 442376 | tf_op jit(solution)/shard_map/ppermute | solution.py:10
  172.3 7.2 %collective-permute-done.4 = bf16[768,96]{0,1:T(8,128)(2,1)} collective-permute-done((bf16[768,96]{0,1:T(8,128)(2,1)}, bf16[768,96]{0,1:T(8,128)(2,1)}, u32[]{:S(2)}, u32[]{:S(2)}) %collective-permute-start.4) | collective-permute-done | bytes 147488 | tf_op jit(solution)/shard_map/ppermute | solution.py:10
  181.5 44.0 %collective-permute-done.3 = bf16[768,768]{0,1:T(8,128)(2,1)} collective-permute-done((bf16[768,768]{0,1:T(8,128)(2,1)S(1)}, bf16[768,768]{0,1:T(8,128)(2,1)}, u32[]{:S(2)}, u32[]{:S(2)}) %collective-permute-start.3) | collective-permute-done | bytes 1179680 | tf_op jit(solution)/shard_map/ppermute | solution.py:10
  225.6 3.4 fusion.1
  228.9 4.0 fusion.57
  232.9 11.3 %collective-permute-start.6 = (bf16[768,96]{0,1:T(8,128)(2,1)}, bf16[768,96]{0,1:T(8,128)(2,1)}, u32[]{:S(2)}, u32[]{:S(2)}) collective-permute-start(bf16[768,96]{0,1:T(8,128)(2,1)} %get-tuple-element.8), channel_id=1, source_target_pairs={{64,0},{72,8},{80,16},{88,24},{96,32},{104,40},{112,48},{120,56},{... | collective-permute-start | bytes 442376 | tf_op jit(solution)/shard_map/ppermute | solution.py:10
  244.3 3.0 collective-permute-done.6
  247.4 9.2 %collective-permute-start.5 = (bf16[768,768]{0,1:T(8,128)(2,1)S(1)}, bf16[768,768]{0,1:T(8,128)(2,1)}, u32[]{:S(2)}, u32[]{:S(2)}) collective-permute-start(bf16[768,768]{0,1:T(8,128)(2,1)S(1)} %copy-done.3), channel_id=1, source_target_pairs={{32,0},{40,8},{48,16},{56,24},{64,32},{72,40},{80,48},{88,56},{96,... | collective-permute-start | bytes 3538952 | tf_op jit(solution)/shard_map/ppermute | solution.py:10
  256.5 51.7 %collective-permute-done.5 = bf16[768,768]{0,1:T(8,128)(2,1)} collective-permute-done((bf16[768,768]{0,1:T(8,128)(2,1)S(1)}, bf16[768,768]{0,1:T(8,128)(2,1)}, u32[]{:S(2)}, u32[]{:S(2)}) %collective-permute-start.5) | collective-permute-done | bytes 1179680 | tf_op jit(solution)/shard_map/ppermute | solution.py:10
  308.2 3.4 fusion.2
  311.6 4.0 fusion.60
  317.6 9.2 %collective-permute-done.8 = bf16[768,96]{0,1:T(8,128)(2,1)} collective-permute-done((bf16[768,96]{0,1:T(8,128)(2,1)}, bf16[768,96]{0,1:T(8,128)(2,1)}, u32[]{:S(2)}, u32[]{:S(2)}) %collective-permute-start.8) | collective-permute-done | bytes 147488 | tf_op jit(solution)/shard_map/ppermute | solution.py:10
  326.9 4.9 collective-permute-start.7
  331.8 24.2 %collective-permute-done.7 = bf16[768,768]{0,1:T(8,128)(2,1)S(1)} collective-permute-done((bf16[768,768]{0,1:T(8,128)(2,1)S(1)}, bf16[768,768]{0,1:T(8,128)(2,1)S(1)}, u32[]{:S(2)}, u32[]{:S(2)}) %collective-permute-start.7) | collective-permute-done | bytes 1179680 | tf_op jit(solution)/shard_map/ppermute | solution.py:10
  358.8 4.3 collective-permute-start.9
  363.2 3.5 fusion.63
  368.0 13.3 %collective-permute-done.10 = bf16[768,96]{0,1:T(8,128)(2,1)} collective-permute-done((bf16[768,96]{0,1:T(8,128)(2,1)}, bf16[768,96]{0,1:T(8,128)(2,1)}, u32[]{:S(2)}, u32[]{:S(2)}) %collective-permute-start.10) | collective-permute-done | bytes 147488 | tf_op jit(solution)/shard_map/ppermute | solution.py:10
  381.3 66.8 %collective-permute-done.9 = bf16[768,768]{0,1:T(8,128)(2,1)} collective-permute-done((bf16[768,768]{0,1:T(8,128)(2,1)S(1)}, bf16[768,768]{0,1:T(8,128)(2,1)}, u32[]{:S(2)}, u32[]{:S(2)}) %collective-permute-start.9) | collective-permute-done | bytes 1179680 | tf_op jit(solution)/shard_map/ppermute | solution.py:10
  448.0 3.1 fusion.4
  452.4 53.9 %collective-permute-done.11 = bf16[768,768]{0,1:T(8,128)(2,1)} collective-permute-done((bf16[768,768]{0,1:T(8,128)(2,1)S(1)}, bf16[768,768]{0,1:T(8,128)(2,1)}, u32[]{:S(2)}, u32[]{:S(2)}) %collective-permute-start.11) | collective-permute-done | bytes 1179680 | tf_op jit(solution)/shard_map/ppermute | solution.py:10
  508.5 3.4 fusion.11
  (45 shorter events, 23.8 us)
Async XLA Ops:
  7.2 3.6 copy-start
  7.2 34.2 %all-gather.24.cloned.1.call-start = ((), (), s32[]{:S(2)}) async-start(), calls=%async_computation.7 | async-start | bytes 1327104 | tf_op jit(solution)/shard_map/all_gather | solution.py:30
  9.0 63.6 %all-gather.10.cloned.1.call-start = ((), (), s32[]{:S(2)}) async-start(), calls=%async_computation | async-start | bytes 1327104 | tf_op jit(solution)/shard_map/all_gather | solution.py:21
  10.7 102.5 %all-gather.12.cloned.1.call-start = ((), (), s32[]{:S(2)}) async-start(), calls=%async_computation.1 | async-start | bytes 1327104 | tf_op jit(solution)/shard_map/all_gather | solution.py:46
  44.6 68.6 %copy-start.1 = (bf16[1,768,768]{1,2,0:T(8,128)(2,1)S(1)}, bf16[1,768,768]{1,2,0:T(8,128)(2,1)}, u32[]{:S(2)}) copy-start(bf16[1,768,768]{1,2,0:T(8,128)(2,1)} %all-gather.24.cloned.1.call-done) | copy-start | bytes 3538948
  76.0 7.2 %collective-permute-start = (bf16[768,96]{0,1:T(8,128)(2,1)S(1)}, bf16[768,96]{0,1:T(8,128)(2,1)}, u32[]{:S(2)}, u32[]{:S(2)}) collective-permute-start(bf16[768,96]{0,1:T(8,128)(2,1)S(1)} %get-tuple-element.2), channel_id=1, source_target_pairs={{8,0},{16,8},{24,16},{32,24},{40,32},{48,40},{56,48},{64,56},{72,6... | collective-permute-start | bytes 442376 | tf_op jit(solution)/shard_map/ppermute | solution.py:10
  83.1 78.0 %all-gather.14.cloned.1.call-start = ((), (), s32[]{:S(2)}) async-start(), calls=%async_computation.2 | async-start | bytes 1327104 | tf_op jit(solution)/shard_map/all_gather | solution.py:46
  116.7 12.6 %collective-permute-start.2 = (bf16[768,96]{0,1:T(8,128)(2,1)}, bf16[768,96]{0,1:T(8,128)(2,1)}, u32[]{:S(2)}, u32[]{:S(2)}) collective-permute-start(bf16[768,96]{0,1:T(8,128)(2,1)} %get-tuple-element.4), channel_id=1, source_target_pairs={{16,0},{24,8},{32,16},{40,24},{48,32},{56,40},{64,48},{72,56},{80,... | collective-permute-start | bytes 442376 | tf_op jit(solution)/shard_map/ppermute | solution.py:10
  129.3 99.6 %all-gather.16.cloned.1.call-start = ((), (), s32[]{:S(2)}) async-start(), calls=%async_computation.3 | async-start | bytes 1327104 | tf_op jit(solution)/shard_map/all_gather | solution.py:46
  129.4 28.4 %collective-permute-start.1 = (bf16[768,768]{0,1:T(8,128)(2,1)S(1)}, bf16[768,768]{0,1:T(8,128)(2,1)}, u32[]{:S(2)}, u32[]{:S(2)}) collective-permute-start(bf16[768,768]{0,1:T(8,128)(2,1)S(1)} %bitcast.60), channel_id=1, source_target_pairs={{8,0},{16,8},{24,16},{32,24},{40,32},{48,40},{56,48},{64,56},{72,6... | collective-permute-start | bytes 3538952 | tf_op jit(solution)/shard_map/ppermute | solution.py:10
  161.1 18.5 %copy-start.2 = (bf16[768,768]{0,1:T(8,128)(2,1)S(1)}, bf16[768,768]{0,1:T(8,128)(2,1)}, u32[]{:S(2)}) copy-start(bf16[768,768]{0,1:T(8,128)(2,1)} %fusion) | copy-start | bytes 3538948
  165.1 14.4 %collective-permute-start.4 = (bf16[768,96]{0,1:T(8,128)(2,1)}, bf16[768,96]{0,1:T(8,128)(2,1)}, u32[]{:S(2)}, u32[]{:S(2)}) collective-permute-start(bf16[768,96]{0,1:T(8,128)(2,1)} %get-tuple-element.6), channel_id=1, source_target_pairs={{32,0},{40,8},{48,16},{56,24},{64,32},{72,40},{80,48},{88,56},{96,... | collective-permute-start | bytes 442376 | tf_op jit(solution)/shard_map/ppermute | solution.py:10
  179.5 132.1 %all-gather.18.cloned.1.call-start = ((), (), s32[]{:S(2)}) async-start(), calls=%async_computation.4 | async-start | bytes 1327104 | tf_op jit(solution)/shard_map/all_gather | solution.py:46
  179.6 46.0 %collective-permute-start.3 = (bf16[768,768]{0,1:T(8,128)(2,1)S(1)}, bf16[768,768]{0,1:T(8,128)(2,1)}, u32[]{:S(2)}, u32[]{:S(2)}) collective-permute-start(bf16[768,768]{0,1:T(8,128)(2,1)S(1)} %copy-done.2), channel_id=1, source_target_pairs={{16,0},{24,8},{32,16},{40,24},{48,32},{56,40},{64,48},{72,56},{80,... | collective-permute-start | bytes 3538952 | tf_op jit(solution)/shard_map/ppermute | solution.py:10
  228.9 18.4 %copy-start.3 = (bf16[768,768]{0,1:T(8,128)(2,1)S(1)}, bf16[768,768]{0,1:T(8,128)(2,1)}, u32[]{:S(2)}) copy-start(bf16[768,768]{0,1:T(8,128)(2,1)} %fusion.1) | copy-start | bytes 3538948
  232.9 14.4 %collective-permute-start.6 = (bf16[768,96]{0,1:T(8,128)(2,1)}, bf16[768,96]{0,1:T(8,128)(2,1)}, u32[]{:S(2)}, u32[]{:S(2)}) collective-permute-start(bf16[768,96]{0,1:T(8,128)(2,1)} %get-tuple-element.8), channel_id=1, source_target_pairs={{64,0},{72,8},{80,16},{88,24},{96,32},{104,40},{112,48},{120,56},{... | collective-permute-start | bytes 442376 | tf_op jit(solution)/shard_map/ppermute | solution.py:10
  247.3 115.9 %all-gather.20.cloned.1.call-start = ((), (), s32[]{:S(2)}) async-start(), calls=%async_computation.5 | async-start | bytes 1327104 | tf_op jit(solution)/shard_map/all_gather | solution.py:46
  247.4 60.9 %collective-permute-start.5 = (bf16[768,768]{0,1:T(8,128)(2,1)S(1)}, bf16[768,768]{0,1:T(8,128)(2,1)}, u32[]{:S(2)}, u32[]{:S(2)}) collective-permute-start(bf16[768,768]{0,1:T(8,128)(2,1)S(1)} %copy-done.3), channel_id=1, source_target_pairs={{32,0},{40,8},{48,16},{56,24},{64,32},{72,40},{80,48},{88,56},{96,... | collective-permute-start | bytes 3538952 | tf_op jit(solution)/shard_map/ppermute | solution.py:10
  311.6 15.3 %copy-start.5 = (bf16[768,768]{0,1:T(8,128)(2,1)S(1)}, bf16[768,768]{0,1:T(8,128)(2,1)}, u32[]{:S(2)}) copy-start(bf16[768,768]{0,1:T(8,128)(2,1)} %fusion.2) | copy-start | bytes 3538948
  315.6 11.2 %collective-permute-start.8 = (bf16[768,96]{0,1:T(8,128)(2,1)}, bf16[768,96]{0,1:T(8,128)(2,1)}, u32[]{:S(2)}, u32[]{:S(2)}) collective-permute-start(bf16[768,96]{0,1:T(8,128)(2,1)} %get-tuple-element.10), channel_id=1, source_target_pairs={{128,0},{136,8},{144,16},{152,24},{160,32},{168,40},{176,48},{184,... | collective-permute-start | bytes 442376 | tf_op jit(solution)/shard_map/ppermute | solution.py:10
  326.8 181.7 %all-gather.22.cloned.1.call-start = ((), (), s32[]{:S(2)}) async-start(), calls=%async_computation.6 | async-start | bytes 1327104 | tf_op jit(solution)/shard_map/all_gather | solution.py:46
  326.9 29.2 %collective-permute-start.7 = (bf16[768,768]{0,1:T(8,128)(2,1)S(1)}, bf16[768,768]{0,1:T(8,128)(2,1)S(1)}, u32[]{:S(2)}, u32[]{:S(2)}) collective-permute-start(bf16[768,768]{0,1:T(8,128)(2,1)S(1)} %copy-done.5), channel_id=1, source_target_pairs={{64,0},{72,8},{80,16},{88,24},{96,32},{104,40},{112,48},{120,56},{... | collective-permute-start | bytes 3538952 | tf_op jit(solution)/shard_map/ppermute | solution.py:10
  358.8 7.9 %copy-start.4 = (bf16[768,768]{0,1:T(8,128)(2,1)}, bf16[768,768]{0,1:T(8,128)(2,1)S(1)}, u32[]{:S(2)}) copy-start(bf16[768,768]{0,1:T(8,128)(2,1)S(1)} %fusion.3) | copy-start | bytes 3538948
  358.8 89.2 %collective-permute-start.9 = (bf16[768,768]{0,1:T(8,128)(2,1)S(1)}, bf16[768,768]{0,1:T(8,128)(2,1)}, u32[]{:S(2)}, u32[]{:S(2)}) collective-permute-start(bf16[768,768]{0,1:T(8,128)(2,1)S(1)} %fusion.3), channel_id=1, source_target_pairs={{128,0},{136,8},{144,16},{152,24},{160,32},{168,40},{176,48},{184,... | collective-permute-start | bytes 3538952 | tf_op jit(solution)/shard_map/ppermute | solution.py:10
  366.7 14.6 %collective-permute-start.10 = (bf16[768,96]{0,1:T(8,128)(2,1)}, bf16[768,96]{0,1:T(8,128)(2,1)}, u32[]{:S(2)}, u32[]{:S(2)}) collective-permute-start(bf16[768,96]{0,1:T(8,128)(2,1)} %get-tuple-element.12), channel_id=1, source_target_pairs={{256,0},{264,8},{272,16},{280,24},{288,32},{296,40},{304,48},{312,... | collective-permute-start | bytes 442376 | tf_op jit(solution)/shard_map/ppermute | solution.py:10
  451.1 55.2 %collective-permute-start.11 = (bf16[768,768]{0,1:T(8,128)(2,1)S(1)}, bf16[768,768]{0,1:T(8,128)(2,1)}, u32[]{:S(2)}, u32[]{:S(2)}) collective-permute-start(bf16[768,768]{0,1:T(8,128)(2,1)S(1)} %fusion.4), channel_id=1, source_target_pairs={{256,0},{264,8},{272,16},{280,24},{288,32},{296,40},{304,48},{312,... | collective-permute-start | bytes 3538952 | tf_op jit(solution)/shard_map/ppermute | solution.py:10
Sparse Core Ops, SparseCore 0:
  10.7 30.6 all-gather.23
  43.5 29.0 all-gather.9
  83.3 29.8 all-gather.11
  129.4 29.2 all-gather.13
  179.6 31.5 all-gather.15
  247.4 36.2 all-gather.17
  326.9 32.7 all-gather.19
  381.4 92.9 all-gather.21
where the time goes:
time: 520 us; the launch traced here: 519 us
  waiting for transfers between devices  402 us (77%)
  starting transfers between devices  50.1 us (10%)
  matrix products  49.2 us (9%)
  between operations  14.4 us (3%)
    ppermute x12, waiting for transfers between devices, passed_along(): return lax.ppermute(block, axis, route)  315 us
    ppermute x12, starting transfers between devices, passed_along(): return lax.ppermute(block, axis, route)  49.7 us
    all_gather x6, waiting for transfers between devices, shards(): partner_cov = lax.all_gather(incoming, 'panel', axis=1, tiled=True)  30 us
    all_gather x1, waiting for transfers between devices, shards(): full_coupling = lax.all_gather(own_part, 'panel', axis=1, tiled=True)  28.5 us
    all_gather x1, waiting for transfers between devices, shards(): lax.all_gather(factor_cols.astype(jnp.bfloat16), 'panel', axis=1, tiled=T...  28 us
    dot_general x6, matrix products, shards(): lax.dot_general(composite, middle, (((0,), (0,)), ((), ())), preferred_el...  22.3 us
    dot_general x5, matrix products, shards(): jnp.dot(partner_comp, composite, preferred_element_type=jnp.float32)  15.9 us
  transfers between devices with their start and end apart: 20, of which 15 were waited for; matrix products, arithmetic and copies ran while one was open for 6% of the time, Pallas kernels for 0%

commit v1 on v0

v1 whole, which is shorter than its diff:
```python
import functools

import jax
import jax.numpy as jnp
from jax import lax
from jax.experimental import pallas as pl
from jax.experimental.pallas import tpu as pltpu
from jax.sharding import PartitionSpec as P

MESH = pl.DeviceIdType.MESH
F32 = jnp.float32
BF16 = jnp.bfloat16


def dot(a, b):
    return jnp.dot(a, b, preferred_element_type=F32)


def dot_nt(a, b):
    return lax.dot_general(a, b, (((1,), (1,)), ((), ())), preferred_element_type=F32)


def split(a):
    high = a.astype(BF16)
    return high, (a - high.astype(F32)).astype(BF16)


def kernel(
    steps, chips, rounds,
    factor_ref, coupling_ref, sigma_ref, cov_out, prop_out,
    comp, comp_t, fac_t, own_cov, cov_send, comp_recv, cov_recv, blocks, gathered, sigma_buf,
    g_send, g_recv, t_send, t_recv, a_send, a_recv, sigma_sem,
):
    width, n = own_cov.shape
    panels = 2 * chips
    t = lax.axis_index("tm")
    p = lax.axis_index("panel")
    x, c = lax.div(p, 2), lax.rem(p, 2)
    sibling = 2 * x + 1 - c
    last = t == steps - 1
    pending = []

    def has_source(r):
        return t + (1 << r) < steps

    def has_target(r):
        return t - (1 << r) >= 0

    def rows(q):
        return pl.ds(pl.multiple_of(q * width, 32), width)

    def away(dx, core):
        return 2 * lax.rem(x + chips + dx, chips) + core

    def send(cond, make):
        make().start()
        pending.append((cond, make))

    def copy(src, dst, s, r, tm, panel):
        return pltpu.make_async_remote_copy(
            src_ref=src, dst_ref=dst, send_sem=s, recv_sem=r, device_id=(tm, panel), device_id_type=MESH
        )

    def gather_copy(k, buf, q, i, to):
        return copy(buf().at[rows(q)], buf().at[rows(q)], g_send.at[k, i], g_recv.at[k, i], t, to)

    def start_gather(k, buf, cond=None):
        for dx in (2, 1, 3)[: chips - 1] if chips > 2 else (1,):
            send(cond, lambda dx=dx: gather_copy(k, buf, p, dx - 1, away(dx, c)))
        send(cond, lambda: gather_copy(k, buf, p, 3, sibling))

    def finish_gather(k, buf, cond=None):
        for dx in (1, 3, 2)[: chips - 1] if chips > 2 else (1,):
            gather_copy(k, buf, away(-dx, c), dx - 1, sibling).wait_recv()
            send(cond, lambda dx=dx: gather_copy(k, buf, away(-dx, c), 3 + dx, sibling))
        gather_copy(k, buf, sibling, 3, sibling).wait_recv()
        for dx in (1, 3, 2)[: chips - 1] if chips > 2 else (1,):
            gather_copy(k, buf, away(-dx, 1 - c), 3 + dx, sibling).wait_recv()

    def exchange_copy(k, src, dst, j, to):
        return copy(blocks.at[k, src], gathered.at[k, rows(dst)], a_send.at[k, j - 1], a_recv.at[k, j - 1], t, to)

    def start_exchange(k, panel, cond=None):
        wide = jnp.concatenate([panel, panel[:, :128]], axis=1)
        for q in range(panels):
            blocks[k, q] = wide[:, q * width : q * width + 128]
        for j in range(1, panels):
            q = lambda j=j: lax.rem(p + j, panels)
            send(cond, lambda j=j, q=q: exchange_copy(k, q(), p, j, q()))
        gathered[k, rows(p)] = blocks[k, p]

    def finish_exchange(k):
        for j in range(1, panels):
            q = lax.rem(p + panels - j, panels)
            exchange_copy(k, q, q, j, q).wait_recv()

    def comp_copy(r, to):
        return copy(comp.at[r, rows(p)], comp_recv.at[r], t_send.at[r, 0], t_recv.at[r, 0], to, p)

    def cov_copy(r, to):
        return copy(cov_send.at[r], cov_recv.at[r], t_send.at[r, 1], t_recv.at[r, 1], to, p)

    def send_comp(r):
        @pl.when(has_target(r))
        def _():
            send(lambda: has_target(r), lambda: comp_copy(r, t - (1 << r)))

    def send_cov(r):
        cov_send[r] = own_cov[...].astype(BF16)

        @pl.when(has_target(r))
        def _():
            send(lambda: has_target(r), lambda: cov_copy(r, t - (1 << r)))

    @pl.when(last)
    def _():
        pltpu.make_async_copy(sigma_ref, sigma_buf, sigma_sem).start()

    barrier = pltpu.get_barrier_semaphore()
    for j in range(1, panels):
        pl.semaphore_signal(barrier, 1, device_id=(t, lax.rem(p + j, panels)), device_id_type=MESH)
    for r in range(rounds):
        @pl.when(has_target(r))
        def _():
            pl.semaphore_signal(barrier, 1, device_id=(t - (1 << r), p), device_id_type=MESH)

        @pl.when(has_source(r))
        def _():
            pl.semaphore_signal(barrier, 1, device_id=(t + (1 << r), p), device_id_type=MESH)

    comp_t[rows(p)] = coupling_ref[...].T.astype(BF16)
    fac_high, fac_low = split(factor_ref[...].T)
    fac_t[rows(p)] = fac_high

    peers = panels - 1
    for r in range(rounds):
        peers += has_target(r).astype(jnp.int32) + has_source(r).astype(jnp.int32)
    pl.semaphore_wait(barrier, peers)

    start_gather(rounds, lambda: comp_t)
    start_gather(0, lambda: fac_t)
    finish_gather(rounds, lambda: comp_t)
    for j in range(n // 128):
        comp[0, :, 128 * j : 128 * (j + 1)] = comp_t[128 * j : 128 * (j + 1), :].T
    send_comp(0)
    finish_gather(0, lambda: fac_t)
    own_cov[...] = dot_nt(fac_high, fac_t[...]) + dot_nt(fac_low, fac_t[...])

    @pl.when(last)
    def _():
        pltpu.make_async_copy(sigma_ref, sigma_buf, sigma_sem).wait()
        sig_high, sig_low = split(sigma_buf[...])
        own = comp_t[rows(p)]
        w_high, w_low = split(dot(own, sig_high) + dot(own, sig_low))
        own_cov[...] += dot(w_high, comp[0]) + dot(w_low, comp[0])

    send_cov(0)

    for r in range(rounds):
        active = has_source(r)
        more = r + 1 < rounds
        if r:
            @pl.when(active)
            def _():
                finish_gather(r, lambda r=r: comp.at[r], lambda r=r: has_source(r))

        if more:
            @pl.when(active)
            def _():
                comp_copy(r, t).wait_recv()
                comp[r + 1, rows(p)] = dot(comp_recv[r], comp[r]).astype(BF16)

            @pl.when(jnp.logical_not(active))
            def _():
                comp[r + 1, rows(p)] = comp[r, rows(p)]

            send_comp(r + 1)

            @pl.when(has_source(r + 1))
            def _():
                start_gather(r + 1, lambda r=r: comp.at[r + 1], lambda r=r: has_source(r + 1))
        else:
            @pl.when(active)
            def _():
                comp_copy(r, t).wait_recv()
                start_exchange(rounds, dot(comp_recv[r], comp[r]).astype(BF16), lambda r=r: has_source(r))

            @pl.when(jnp.logical_not(active))
            def _():
                start_exchange(rounds, comp[r, rows(p)], lambda r=r: jnp.logical_not(has_source(r)))

        @pl.when(active)
        def _():
            cov_copy(r, t).wait_recv()
            start_exchange(r, dot(cov_recv[r], comp[r]).astype(BF16), lambda r=r: has_source(r))
            finish_exchange(r)
            middle_t = gathered[r].T[:width]
            own_cov[...] += dot(middle_t, comp[r])

        if more:
            send_cov(r + 1)

    cov_out[...] = own_cov[...].T
    finish_exchange(rounds)
    prop_out[...] = gathered[rounds][:, :width]

    for cond, make in pending:
        if cond is None:
            make().wait_send()
        else:
            pl.when(cond())(lambda make=make: make().wait_send())


def shards(factor_inverse, coupling, sigma_after):
    steps, panels = lax.axis_size("tm"), lax.axis_size("panel")
    n, width = factor_inverse.shape[1:]
    rounds = (steps - 1).bit_length()
    chips = panels // 2
    vmem = pl.BlockSpec(memory_space=pltpu.VMEM)
    cov, prop = pl.pallas_call(
        functools.partial(kernel, steps, chips, rounds),
        out_shape=(
            jax.ShapeDtypeStruct((n, width), F32),
            jax.ShapeDtypeStruct((n, width), BF16),
        ),
        in_specs=[vmem, vmem, pl.BlockSpec(memory_space=pl.ANY)],
        out_specs=(vmem, vmem),
        scratch_shapes=[
            pltpu.VMEM((rounds, n, n), BF16),
            pltpu.VMEM((n, n), BF16),
            pltpu.VMEM((n, n), BF16),
            pltpu.VMEM((width, n), F32),
            pltpu.VMEM((rounds, width, n), BF16),
            pltpu.VMEM((rounds, width, n), BF16),
            pltpu.VMEM((rounds, width, n), BF16),
            pltpu.VMEM((rounds + 1, panels, width, 128), BF16),
            pltpu.VMEM((rounds + 1, n, 128), BF16),
            pltpu.VMEM((n, n), F32),
            pltpu.SemaphoreType.DMA((rounds + 1, 7)),
            pltpu.SemaphoreType.DMA((rounds + 1, 7)),
            pltpu.SemaphoreType.DMA((rounds, 2)),
            pltpu.SemaphoreType.DMA((rounds, 2)),
            pltpu.SemaphoreType.DMA((rounds + 1, panels - 1)),
            pltpu.SemaphoreType.DMA((rounds + 1, panels - 1)),
            pltpu.SemaphoreType.DMA,
        ],
        compiler_params=pltpu.CompilerParams(
            collective_id=0, has_side_effects=True, vmem_limit_bytes=48 << 20
        ),
        name="scan",
    )(factor_inverse[0], coupling[0], sigma_after)
    return cov[None], prop[None]


def solution(mesh):
    placed = (P("tm", None, "panel"), P("tm", None, "panel"), P())
    return jax.shard_map(
        shards,
        mesh=mesh,
        in_specs=placed,
        out_specs=(P("tm", None, "panel"), P("tm", None, "panel")),
        check_vma=False,
    )
```

time: 520 us -> 128 us (0.25)
  the two profiles are of different devices: /device:TPU:151 before, /device:TPU:65 now
where the time goes in v1:
time: 128 us
  Pallas kernels  121 us (95%)
  local copies, waits for them, and re-layouts  5.59 us (4%)
    pallas_call x1, Pallas kernels, shards(): pl.pallas_call(functools.partial(kernel, steps, chips, rounds), out_shape...  121 us
    unnamed x6, local copies, waits for them, and re-layouts  5.59 us

profile of v1, /device:TPU:65, one launch (start us, length us, event | category | flops | bytes accessed | tf_op | source)
XLA Modules:
  0.0 127.5 jit_solution(18257497253567192871)
XLA Ops:
  0.6 1.1 copy.5
  1.8 1.1 copy.6
  2.9 0.0 copy-start
  2.9 1.7 %copy-done = f32[768,768]{1,0:T(8,128)S(1)} copy-done((f32[768,768]{1,0:T(8,128)S(1)}, f32[768,768]{1,0:T(8,128)}, u32[]{:S(2)}) %copy-start) | copy-done | bytes 2359320
  4.6 121.3 %scan.1 = (f32[768,96]{1,0:T(8,128)S(1)}, bf16[768,96]{1,0:T(8,128)(2,1)S(1)}) custom-call(f32[768,96]{1,0:T(8,128)S(1)} %bitcast.4, f32[768,96]{1,0:T(8,128)S(1)} %bitcast.5, f32[768,768]{1,0:T(8,128)S(1)} %copy-done), custom_call_target="tpu_custom_call" | custom-call | tf_op jit(solution)/shard_map/scan/pallas_call | solution.py:220
  125.8 0.9 copy.7
  126.7 0.8 copy.8
Async XLA Ops:
  2.9 1.7 %copy-start = (f32[768,768]{1,0:T(8,128)S(1)}, f32[768,768]{1,0:T(8,128)}, u32[]{:S(2)}) copy-start(f32[768,768]{1,0:T(8,128)} %sigma_ref.1) | copy-start | bytes 7077892

commit v2 on v1

--- a/solution.py
+++ b/solution.py
@@ -28,8 +28,8 @@
 def kernel(
     steps, chips, rounds,
     factor_ref, coupling_ref, sigma_ref, cov_out, prop_out,
-    comp, comp_t, fac_t, own_cov, cov_send, comp_recv, cov_recv, blocks, gathered, sigma_buf,
-    g_send, g_recv, t_send, t_recv, a_send, a_recv, sigma_sem,
+    comp, comp_t, fac_t, coupling_buf, factor_buf, own_cov, cov_send, comp_recv, cov_recv, blocks, gathered, sigma_buf,
+    g_send, g_recv, t_send, t_recv, a_send, a_recv, load_sem,
 ):
     width, n = own_cov.shape
     panels = 2 * chips
@@ -84,7 +84,7 @@
         wide = jnp.concatenate([panel, panel[:, :128]], axis=1)
         for q in range(panels):
             blocks[k, q] = wide[:, q * width : q * width + 128]
-        for j in range(1, panels):
+        for j in sorted(range(1, panels), key=lambda j: abs(j - chips)):
             q = lambda j=j: lax.rem(p + j, panels)
             send(cond, lambda j=j, q=q: exchange_copy(k, q(), p, j, q()))
         gathered[k, rows(p)] = blocks[k, p]
@@ -112,9 +112,16 @@
         def _():
             send(lambda: has_target(r), lambda: cov_copy(r, t - (1 << r)))
 
+    loads = [
+        pltpu.make_async_copy(coupling_ref, coupling_buf, load_sem.at[0]),
+        pltpu.make_async_copy(factor_ref, factor_buf, load_sem.at[1]),
+    ]
+    for load in loads:
+        load.start()
+
     @pl.when(last)
     def _():
-        pltpu.make_async_copy(sigma_ref, sigma_buf, sigma_sem).start()
+        pltpu.make_async_copy(sigma_ref, sigma_buf, load_sem.at[2]).start()
 
     barrier = pltpu.get_barrier_semaphore()
     for j in range(1, panels):
@@ -128,8 +135,10 @@
         def _():
             pl.semaphore_signal(barrier, 1, device_id=(t + (1 << r), p), device_id_type=MESH)
 
-    comp_t[rows(p)] = coupling_ref[...].T.astype(BF16)
-    fac_high, fac_low = split(factor_ref[...].T)
+    loads[0].wait()
+    comp_t[rows(p)] = coupling_buf[...].astype(BF16)
+    loads[1].wait()
+    fac_high, fac_low = split(factor_buf[...])
     fac_t[rows(p)] = fac_high
 
     peers = panels - 1
@@ -148,7 +157,7 @@
 
     @pl.when(last)
     def _():
-        pltpu.make_async_copy(sigma_ref, sigma_buf, sigma_sem).wait()
+        pltpu.make_async_copy(sigma_ref, sigma_buf, load_sem.at[2]).wait()
         sig_high, sig_low = split(sigma_buf[...])
         own = comp_t[rows(p)]
         w_high, w_low = split(dot(own, sig_high) + dot(own, sig_low))
@@ -200,9 +209,9 @@
         if more:
             send_cov(r + 1)
 
-    cov_out[...] = own_cov[...].T
+    cov_out[...] = own_cov[...]
     finish_exchange(rounds)
-    prop_out[...] = gathered[rounds][:, :width]
+    prop_out[...] = gathered[rounds].T[:width]
 
     for cond, make in pending:
         if cond is None:
@@ -220,15 +229,17 @@
     cov, prop = pl.pallas_call(
         functools.partial(kernel, steps, chips, rounds),
         out_shape=(
-            jax.ShapeDtypeStruct((n, width), F32),
-            jax.ShapeDtypeStruct((n, width), BF16),
+            jax.ShapeDtypeStruct((width, n), F32),
+            jax.ShapeDtypeStruct((width, n), BF16),
         ),
-        in_specs=[vmem, vmem, pl.BlockSpec(memory_space=pl.ANY)],
+        in_specs=[pl.BlockSpec(memory_space=pl.ANY)] * 3,
         out_specs=(vmem, vmem),
         scratch_shapes=[
             pltpu.VMEM((rounds, n, n), BF16),
             pltpu.VMEM((n, n), BF16),
             pltpu.VMEM((n, n), BF16),
+            pltpu.VMEM((width, n), F32),
+            pltpu.VMEM((width, n), F32),
             pltpu.VMEM((width, n), F32),
             pltpu.VMEM((rounds, width, n), BF16),
             pltpu.VMEM((rounds, width, n), BF16),
@@ -242,14 +253,14 @@
             pltpu.SemaphoreType.DMA((rounds, 2)),
             pltpu.SemaphoreType.DMA((rounds + 1, panels - 1)),
             pltpu.SemaphoreType.DMA((rounds + 1, panels - 1)),
-            pltpu.SemaphoreType.DMA,
+            pltpu.SemaphoreType.DMA((3,)),
         ],
         compiler_params=pltpu.CompilerParams(
-            collective_id=0, has_side_effects=True, vmem_limit_bytes=48 << 20
+            collective_id=0, has_side_effects=True, vmem_limit_bytes=60 << 20
         ),
         name="scan",
-    )(factor_inverse[0], coupling[0], sigma_after)
-    return cov[None], prop[None]
+    )(factor_inverse[0].T, coupling[0].T, sigma_after)
+    return cov.T[None], prop.T[None]
 
 
 def solution(mesh):

time: 128 us -> 128 us (level)
  the two profiles are of different devices: /device:TPU:65 before, /device:TPU:1 now
where the time goes in v2:
time: 128 us
  Pallas kernels  124 us (97%)
  local copies, waits for them, and re-layouts  3.27 us (3%)
    pallas_call x1, Pallas kernels, shards(): pl.pallas_call(functools.partial(kernel, steps, chips, rounds), out_shape...  124 us
    unnamed x2, local copies, waits for them, and re-layouts  3.27 us

profile of v2, /device:TPU:1, one launch (start us, length us, event | category | flops | bytes accessed | tf_op | source)
XLA Modules:
  0.0 127.6 jit_solution(17878579321561915527)
XLA Ops:
  0.6 123.7 %scan.1 = (f32[96,768]{1,0:T(8,128)}, bf16[96,768]{1,0:T(8,128)(2,1)}) custom-call(f32[96,768]{1,0:T(8,128)} %bitcast.12, f32[96,768]{1,0:T(8,128)} %bitcast.13, f32[768,768]{1,0:T(8,128)} %sigma_ref.1), custom_call_target="tpu_custom_call" | custom-call | tf_op jit(solution)/shard_map/scan/pallas_call | solution.py:229
  124.3 1.7 %copy.7 = f32[1,768,96]{1,2,0:T(8,128)} copy(f32[1,768,96]{1,2,0:T(8,128)} %bitcast.14) | data formatting | bytes 589824
  126.0 1.6 %copy.8 = bf16[1,768,96]{1,2,0:T(8,128)(2,1)} copy(bf16[1,768,96]{1,2,0:T(8,128)(2,1)} %bitcast.15) | data formatting | bytes 294912

commit v3 on v2

--- a/solution.py
+++ b/solution.py
@@ -77,6 +77,35 @@
         for dx in (1, 3, 2)[: chips - 1] if chips > 2 else (1,):
             gather_copy(k, buf, away(-dx, 1 - c), 3 + dx, sibling).wait_recv()
 
+    def triangle_copy(xs, q, i, to):
+        first = 2 * width * xs // 128 * 128
+        part = fac_t.at[rows(q), pl.ds(first, n - first)]
+        return copy(part, part, g_send.at[0, i], g_recv.at[0, i], t, to)
+
+    def for_chip(dx, action):
+        for xs in range(chips):
+            cond = lambda xs=xs: lax.rem(x + chips + dx, chips) == xs
+            pl.when(cond())(lambda xs=xs, cond=cond: action(xs, cond))
+
+    def start_triangle():
+        def sends(xs, cond):
+            for dx in (2, 1, 3):
+                send(cond, lambda dx=dx: triangle_copy(xs, p, dx - 1, away(dx, c)))
+            send(cond, lambda: triangle_copy(xs, p, 3, sibling))
+
+        for_chip(0, sends)
+
+    def finish_triangle():
+        def forward(dx, xs, cond):
+            triangle_copy(xs, away(-dx, c), dx - 1, sibling).wait_recv()
+            send(cond, lambda: triangle_copy(xs, away(-dx, c), 3 + dx, sibling))
+
+        for dx in (1, 3, 2):
+            for_chip(-dx, functools.partial(forward, dx))
+        for_chip(0, lambda xs, cond: triangle_copy(xs, sibling, 3, sibling).wait_recv())
+        for dx in (1, 3, 2):
+            for_chip(-dx, lambda xs, cond, dx=dx: triangle_copy(xs, away(-dx, 1 - c), 3 + dx, sibling).wait_recv())
+
     def exchange_copy(k, src, dst, j, to):
         return copy(blocks.at[k, src], gathered.at[k, rows(dst)], a_send.at[k, j - 1], a_recv.at[k, j - 1], t, to)
 
@@ -123,6 +152,7 @@
     def _():
         pltpu.make_async_copy(sigma_ref, sigma_buf, load_sem.at[2]).start()
 
+    fac_t[...] = jnp.zeros_like(fac_t)
     barrier = pltpu.get_barrier_semaphore()
     for j in range(1, panels):
         pl.semaphore_signal(barrier, 1, device_id=(t, lax.rem(p + j, panels)), device_id_type=MESH)
@@ -147,12 +177,12 @@
     pl.semaphore_wait(barrier, peers)
 
     start_gather(rounds, lambda: comp_t)
-    start_gather(0, lambda: fac_t)
+    start_triangle()
     finish_gather(rounds, lambda: comp_t)
     for j in range(n // 128):
         comp[0, :, 128 * j : 128 * (j + 1)] = comp_t[128 * j : 128 * (j + 1), :].T
     send_comp(0)
-    finish_gather(0, lambda: fac_t)
+    finish_triangle()
     own_cov[...] = dot_nt(fac_high, fac_t[...]) + dot_nt(fac_low, fac_t[...])
 
     @pl.when(last)
@@ -256,7 +286,7 @@
             pltpu.SemaphoreType.DMA((3,)),
         ],
         compiler_params=pltpu.CompilerParams(
-            collective_id=0, has_side_effects=True, vmem_limit_bytes=60 << 20
+            collective_id=0, has_side_effects=True, vmem_limit_bytes=55_990_000
         ),
         name="scan",
     )(factor_inverse[0].T, coupling[0].T, sigma_after)

time: 128 us -> 123 us (0.961)
  Pallas kernels: 124 us -> 121 us
  local copies, waits for them, and re-layouts: 3.27 us -> 1.38 us
    pallas_call x1, Pallas kernels: 124 us -> 121 us  [shards(): pl.pallas_call(functools.partial(kernel, steps, chips, rounds), out_shape...]
    unnamed x2, local copies, waits for them, and re-layouts: 3.27 us -> 1.38 us
where the time goes in v3:
time: 123 us
  Pallas kernels  121 us (98%)
  local copies, waits for them, and re-layouts  1.38 us (1%)
    pallas_call x1, Pallas kernels, shards(): pl.pallas_call(functools.partial(kernel, steps, chips, rounds), out_shape...  121 us

profile of v3, /device:TPU:1, one launch (start us, length us, event | category | flops | bytes accessed | tf_op | source)
XLA Modules:
  0.0 123.3 jit_solution(10642674519326595924)
XLA Ops:
  0.6 121.3 %scan.1 = (f32[96,768]{1,0:T(8,128)S(1)}, bf16[96,768]{1,0:T(8,128)(2,1)S(1)}) custom-call(f32[96,768]{1,0:T(8,128)} %bitcast.14, f32[96,768]{1,0:T(8,128)} %bitcast.15, f32[768,768]{1,0:T(8,128)} %sigma_ref.1), custom_call_target="tpu_custom_call" | custom-call | tf_op jit(solution)/shard_map/scan/pallas_call | solution.py:259
  122.0 0.7 copy.7
  122.7 0.7 copy.8

commit v4 on v3

--- a/solution.py
+++ b/solution.py
@@ -61,6 +61,21 @@
             src_ref=src, dst_ref=dst, send_sem=s, recv_sem=r, device_id=(tm, panel), device_id_type=MESH
         )
 
+    def drain(sent):
+        groups = {}
+        for entry in sent:
+            pending.remove(entry)
+            groups.setdefault(entry[0], []).append(entry[1])
+        for cond, makes in groups.items():
+            def waits(makes=makes):
+                for make in makes:
+                    make().wait_send()
+
+            waits() if cond is None else pl.when(cond())(waits)
+
+    source = [lambda r=r: has_source(r) for r in range(rounds)]
+    target = [lambda r=r: has_target(r) for r in range(rounds)]
+
     def gather_copy(k, buf, q, i, to):
         return copy(buf().at[rows(q)], buf().at[rows(q)], g_send.at[k, i], g_recv.at[k, i], t, to)
 
@@ -109,15 +124,21 @@
     def exchange_copy(k, src, dst, j, to):
         return copy(blocks.at[k, src], gathered.at[k, rows(dst)], a_send.at[k, j - 1], a_recv.at[k, j - 1], t, to)
 
-    def start_exchange(k, panel, cond=None):
+    def put_blocks(k, panel):
         wide = jnp.concatenate([panel, panel[:, :128]], axis=1)
         for q in range(panels):
             blocks[k, q] = wide[:, q * width : q * width + 128]
+
+    def send_blocks(k, cond=None):
         for j in sorted(range(1, panels), key=lambda j: abs(j - chips)):
             q = lambda j=j: lax.rem(p + j, panels)
             send(cond, lambda j=j, q=q: exchange_copy(k, q(), p, j, q()))
         gathered[k, rows(p)] = blocks[k, p]
 
+    def start_exchange(k, panel, cond=None):
+        put_blocks(k, panel)
+        send_blocks(k, cond)
+
     def finish_exchange(k):
         for j in range(1, panels):
             q = lax.rem(p + panels - j, panels)
@@ -132,14 +153,14 @@
     def send_comp(r):
         @pl.when(has_target(r))
         def _():
-            send(lambda: has_target(r), lambda: comp_copy(r, t - (1 << r)))
+            send(target[r], lambda: comp_copy(r, t - (1 << r)))
 
     def send_cov(r):
         cov_send[r] = own_cov[...].astype(BF16)
 
         @pl.when(has_target(r))
         def _():
-            send(lambda: has_target(r), lambda: cov_copy(r, t - (1 << r)))
+            send(target[r], lambda: cov_copy(r, t - (1 << r)))
 
     loads = [
         pltpu.make_async_copy(coupling_ref, coupling_buf, load_sem.at[0]),
@@ -198,56 +219,58 @@
     for r in range(rounds):
         active = has_source(r)
         more = r + 1 < rounds
+        old = pending[:-1]
         if r:
             @pl.when(active)
             def _():
-                finish_gather(r, lambda r=r: comp.at[r], lambda r=r: has_source(r))
+                finish_gather(r, lambda r=r: comp.at[r], source[r])
+
+        @pl.when(active)
+        def _():
+            comp_copy(r, t).wait_recv()
+            panel = dot(comp_recv[r], comp[r]).astype(BF16)
+            if more:
+                comp[r + 1, rows(p)] = panel
+            else:
+                put_blocks(rounds, panel)
+
+        @pl.when(jnp.logical_not(active))
+        def _():
+            if more:
+                comp[r + 1, rows(p)] = comp[r, rows(p)]
+            else:
+                put_blocks(rounds, comp[r, rows(p)])
 
         if more:
-            @pl.when(active)
-            def _():
-                comp_copy(r, t).wait_recv()
-                comp[r + 1, rows(p)] = dot(comp_recv[r], comp[r]).astype(BF16)
-
-            @pl.when(jnp.logical_not(active))
-            def _():
-                comp[r + 1, rows(p)] = comp[r, rows(p)]
-
             send_comp(r + 1)
 
             @pl.when(has_source(r + 1))
             def _():
-                start_gather(r + 1, lambda r=r: comp.at[r + 1], lambda r=r: has_source(r + 1))
+                start_gather(r + 1, lambda r=r: comp.at[r + 1], source[r + 1])
         else:
-            @pl.when(active)
-            def _():
-                comp_copy(r, t).wait_recv()
-                start_exchange(rounds, dot(comp_recv[r], comp[r]).astype(BF16), lambda r=r: has_source(r))
-
-            @pl.when(jnp.logical_not(active))
-            def _():
-                start_exchange(rounds, comp[r, rows(p)], lambda r=r: jnp.logical_not(has_source(r)))
+            send_blocks(rounds)
+
+        drain(old)
 
         @pl.when(active)
         def _():
             cov_copy(r, t).wait_recv()
-            start_exchange(r, dot(cov_recv[r], comp[r]).astype(BF16), lambda r=r: has_source(r))
+            start_exchange(r, dot(cov_recv[r], comp[r]).astype(BF16), source[r])
+
+        if not more:
+            finish_exchange(rounds)
+            prop_out[...] = gathered[rounds].T[:width]
+
+        @pl.when(active)
+        def _():
             finish_exchange(r)
-            middle_t = gathered[r].T[:width]
-            own_cov[...] += dot(middle_t, comp[r])
+            own_cov[...] += dot(gathered[r].T[:width], comp[r])
 
         if more:
             send_cov(r + 1)
 
     cov_out[...] = own_cov[...]
-    finish_exchange(rounds)
-    prop_out[...] = gathered[rounds].T[:width]
-
-    for cond, make in pending:
-        if cond is None:
-            make().wait_send()
-        else:
-            pl.when(cond())(lambda make=make: make().wait_send())
+    drain(pending[:])
 
 
 def shards(factor_inverse, coupling, sigma_after):

time: 123 us -> 123 us (level)
  no operation moved by 1% of the time
where the time goes in v4:
time: 123 us
  Pallas kernels  121 us (98%)
  local copies, waits for them, and re-layouts  1.38 us (1%)
    pallas_call x1, Pallas kernels, shards(): pl.pallas_call(functools.partial(kernel, steps, chips, rounds), out_shape...  121 us

profile of v4, /device:TPU:1, one launch (start us, length us, event | category | flops | bytes accessed | tf_op | source)
XLA Modules:
  0.0 123.0 jit_solution(12124610596242193525)
XLA Ops:
  0.6 121.0 %scan.1 = (f32[96,768]{1,0:T(8,128)S(1)}, bf16[96,768]{1,0:T(8,128)(2,1)S(1)}) custom-call(f32[96,768]{1,0:T(8,128)} %bitcast.14, f32[96,768]{1,0:T(8,128)} %bitcast.15, f32[768,768]{1,0:T(8,128)} %sigma_ref.1), custom_call_target="tpu_custom_call" | custom-call | tf_op jit(solution)/shard_map/scan/pallas_call | solution.py:282
  121.6 0.7 copy.7
  122.3 0.7 copy.8

commit v5 on v4

--- a/solution.py
+++ b/solution.py
@@ -84,8 +84,13 @@
             send(cond, lambda dx=dx: gather_copy(k, buf, p, dx - 1, away(dx, c)))
         send(cond, lambda: gather_copy(k, buf, p, 3, sibling))
 
-    def finish_gather(k, buf, cond=None):
-        for dx in (1, 3, 2)[: chips - 1] if chips > 2 else (1,):
+    def near_gather(k, buf, cond=None):
+        for dx in (1, 3):
+            gather_copy(k, buf, away(-dx, c), dx - 1, sibling).wait_recv()
+            send(cond, lambda dx=dx: gather_copy(k, buf, away(-dx, c), 3 + dx, sibling))
+
+    def finish_gather(k, buf, cond=None, order=(2,)):
+        for dx in order:
             gather_copy(k, buf, away(-dx, c), dx - 1, sibling).wait_recv()
             send(cond, lambda dx=dx: gather_copy(k, buf, away(-dx, c), 3 + dx, sibling))
         gather_copy(k, buf, sibling, 3, sibling).wait_recv()
@@ -199,12 +204,13 @@
 
     start_gather(rounds, lambda: comp_t)
     start_triangle()
-    finish_gather(rounds, lambda: comp_t)
+    finish_gather(rounds, lambda: comp_t, None, (1, 3, 2))
     for j in range(n // 128):
         comp[0, :, 128 * j : 128 * (j + 1)] = comp_t[128 * j : 128 * (j + 1), :].T
     send_comp(0)
     finish_triangle()
-    own_cov[...] = dot_nt(fac_high, fac_t[...]) + dot_nt(fac_low, fac_t[...])
+    both = dot_nt(jnp.concatenate([fac_high, fac_low]), fac_t[...])
+    own_cov[...] = both[:width] + both[width:]
 
     @pl.when(last)
     def _():
@@ -256,6 +262,11 @@
         def _():
             cov_copy(r, t).wait_recv()
             start_exchange(r, dot(cov_recv[r], comp[r]).astype(BF16), source[r])
+
+        if more:
+            @pl.when(has_source(r + 1))
+            def _():
+                near_gather(r + 1, lambda r=r: comp.at[r + 1], source[r + 1])
 
         if not more:
             finish_exchange(rounds)

time: 123 us -> 123 us (level)
  no operation moved by 1% of the time
where the time goes in v5:
time: 123 us
  Pallas kernels  121 us (98%)
  local copies, waits for them, and re-layouts  1.38 us (1%)
    pallas_call x1, Pallas kernels, shards(): pl.pallas_call(functools.partial(kernel, steps, chips, rounds), out_shape...  121 us

profile of v5, /device:TPU:1, one launch (start us, length us, event | category | flops | bytes accessed | tf_op | source)
XLA Modules:
  0.0 123.0 jit_solution(14926877632538959575)
XLA Ops:
  0.6 121.0 %scan.1 = (f32[96,768]{1,0:T(8,128)S(1)}, bf16[96,768]{1,0:T(8,128)(2,1)S(1)}) custom-call(f32[96,768]{1,0:T(8,128)} %bitcast.14, f32[96,768]{1,0:T(8,128)} %bitcast.15, f32[768,768]{1,0:T(8,128)} %sigma_ref.1), custom_call_target="tpu_custom_call" | custom-call | tf_op jit(solution)/shard_map/scan/pallas_call | solution.py:293
  121.6 0.7 copy.7
  122.3 0.7 copy.8

commit v6 on v5

--- a/solution.py
+++ b/solution.py
@@ -79,15 +79,19 @@
     def gather_copy(k, buf, q, i, to):
         return copy(buf().at[rows(q)], buf().at[rows(q)], g_send.at[k, i], g_recv.at[k, i], t, to)
 
-    def start_gather(k, buf, cond=None):
-        for dx in (2, 1, 3)[: chips - 1] if chips > 2 else (1,):
+    def start_gather(k, buf, cond=None, direct=False):
+        for dx in (2, 1, 3) if direct else (1, 3):
             send(cond, lambda dx=dx: gather_copy(k, buf, p, dx - 1, away(dx, c)))
         send(cond, lambda: gather_copy(k, buf, p, 3, sibling))
 
     def near_gather(k, buf, cond=None):
-        for dx in (1, 3):
-            gather_copy(k, buf, away(-dx, c), dx - 1, sibling).wait_recv()
-            send(cond, lambda dx=dx: gather_copy(k, buf, away(-dx, c), 3 + dx, sibling))
+        for side in (1, -1):
+            q = lambda side=side: away(side * (2 * c - 1), c)
+            i = lambda side=side: 1 + side * (2 * c - 1)
+            gather_copy(k, buf, q(), i(), sibling).wait_recv()
+            if side == 1:
+                send(cond, lambda q=q: gather_copy(k, buf, q(), 1, away(1 - 2 * c, c)))
+            send(cond, lambda q=q, i=i: gather_copy(k, buf, q(), 4 + i(), sibling))
 
     def finish_gather(k, buf, cond=None, order=(2,)):
         for dx in order:
@@ -202,7 +206,7 @@
         peers += has_target(r).astype(jnp.int32) + has_source(r).astype(jnp.int32)
     pl.semaphore_wait(barrier, peers)
 
-    start_gather(rounds, lambda: comp_t)
+    start_gather(rounds, lambda: comp_t, None, True)
     start_triangle()
     finish_gather(rounds, lambda: comp_t, None, (1, 3, 2))
     for j in range(n // 128):

time: 123 us -> 122 us (level)
    pallas_call x1, Pallas kernels: 121 us -> 120 us  [shards(): pl.pallas_call(functools.partial(kernel, steps, chips, rounds), out_shape...]
where the time goes in v6:
time: 122 us
  Pallas kernels  120 us (98%)
  local copies, waits for them, and re-layouts  1.38 us (1%)
    pallas_call x1, Pallas kernels, shards(): pl.pallas_call(functools.partial(kernel, steps, chips, rounds), out_shape...  120 us

profile of v6, /device:TPU:1, one launch (start us, length us, event | category | flops | bytes accessed | tf_op | source)
XLA Modules:
  0.0 121.6 jit_solution(11609826450041233325)
XLA Ops:
  0.6 119.6 %scan.1 = (f32[96,768]{1,0:T(8,128)S(1)}, bf16[96,768]{1,0:T(8,128)(2,1)S(1)}) custom-call(f32[96,768]{1,0:T(8,128)} %bitcast.14, f32[96,768]{1,0:T(8,128)} %bitcast.15, f32[768,768]{1,0:T(8,128)} %sigma_ref.1), custom_call_target="tpu_custom_call" | custom-call | tf_op jit(solution)/shard_map/scan/pallas_call | solution.py:297
  120.2 0.7 copy.7
  120.9 0.7 copy.8

commit v7 on v6

--- a/solution.py
+++ b/solution.py
@@ -206,9 +206,10 @@
         peers += has_target(r).astype(jnp.int32) + has_source(r).astype(jnp.int32)
     pl.semaphore_wait(barrier, peers)
 
-    start_gather(rounds, lambda: comp_t, None, True)
+    start_gather(rounds, lambda: comp_t)
     start_triangle()
-    finish_gather(rounds, lambda: comp_t, None, (1, 3, 2))
+    near_gather(rounds, lambda: comp_t)
+    finish_gather(rounds, lambda: comp_t)
     for j in range(n // 128):
         comp[0, :, 128 * j : 128 * (j + 1)] = comp_t[128 * j : 128 * (j + 1), :].T
     send_comp(0)

time: 122 us -> 123 us (level)
    pallas_call x1, Pallas kernels: 120 us -> 121 us  [shards(): pl.pallas_call(functools.partial(kernel, steps, chips, rounds), out_shape...]
where the time goes in v7:
time: 123 us
  Pallas kernels  121 us (98%)
  local copies, waits for them, and re-layouts  1.38 us (1%)
    pallas_call x1, Pallas kernels, shards(): pl.pallas_call(functools.partial(kernel, steps, chips, rounds), out_shape...  121 us

profile of v7, /device:TPU:1, one launch (start us, length us, event | category | flops | bytes accessed | tf_op | source)
XLA Modules:
  0.0 123.0 jit_solution(14475088588354205612)
XLA Ops:
  0.6 121.0 %scan.1 = (f32[96,768]{1,0:T(8,128)S(1)}, bf16[96,768]{1,0:T(8,128)(2,1)S(1)}) custom-call(f32[96,768]{1,0:T(8,128)} %bitcast.14, f32[96,768]{1,0:T(8,128)} %bitcast.15, f32[768,768]{1,0:T(8,128)} %sigma_ref.1), custom_call_target="tpu_custom_call" | custom-call | tf_op jit(solution)/shard_map/scan/pallas_call | solution.py:298
  121.6 0.7 copy.7
  122.3 0.7 copy.8

commit v8 on v6

--- a/solution.py
+++ b/solution.py
@@ -80,8 +80,13 @@
         return copy(buf().at[rows(q)], buf().at[rows(q)], g_send.at[k, i], g_recv.at[k, i], t, to)
 
     def start_gather(k, buf, cond=None, direct=False):
-        for dx in (2, 1, 3) if direct else (1, 3):
-            send(cond, lambda dx=dx: gather_copy(k, buf, p, dx - 1, away(dx, c)))
+        if direct:
+            for dx in (2, 1, 3):
+                send(cond, lambda dx=dx: gather_copy(k, buf, p, dx - 1, away(dx, c)))
+        else:
+            for side in (1, -1):
+                way = lambda side=side: side * (1 - 2 * c)
+                send(cond, lambda way=way: gather_copy(k, buf, p, 1 - way(), away(way(), c)))
         send(cond, lambda: gather_copy(k, buf, p, 3, sibling))
 
     def near_gather(k, buf, cond=None):

time: 122 us -> 122 us (level)
  no operation moved by 1% of the time
where the time goes in v8:
time: 122 us
  Pallas kernels  120 us (98%)
  local copies, waits for them, and re-layouts  1.38 us (1%)
    pallas_call x1, Pallas kernels, shards(): pl.pallas_call(functools.partial(kernel, steps, chips, rounds), out_shape...  120 us

profile of v8, /device:TPU:1, one launch (start us, length us, event | category | flops | bytes accessed | tf_op | source)
XLA Modules:
  0.0 121.6 jit_solution(6463743826307357301)
XLA Ops:
  0.6 119.6 %scan.1 = (f32[96,768]{1,0:T(8,128)S(1)}, bf16[96,768]{1,0:T(8,128)(2,1)S(1)}) custom-call(f32[96,768]{1,0:T(8,128)} %bitcast.14, f32[96,768]{1,0:T(8,128)} %bitcast.15, f32[768,768]{1,0:T(8,128)} %sigma_ref.1), custom_call_target="tpu_custom_call" | custom-call | tf_op jit(solution)/shard_map/scan/pallas_call | solution.py:302
  120.2 0.7 copy.7
  120.9 0.7 copy.8
